TPU v7x, 512 devices: a whole 4x4x16 slice. The times are simulated.
512 devices in a mesh: dp: 16 (over z), tensor: 8 (over x, core), vocab: 4 (over y).
Axes of the slice: x: 4, y: 4, z: 16, core: 2. Of those that a mesh axis runs over, the one named last changes fastest.
Arguments:
- features: bfloat16 [1024, 49152], P('dp', ('tensor', 'vocab')), may hold values from -80 to 80
- fc_weight: bfloat16 [49152, 16384], P(('tensor', 'vocab'), 'dp'), may hold values from -1 to 1
- norm_gain: float32 [16384], P('dp'), may hold values from 0.1 to 1.9
- head_weight: bfloat16 [16384, 16384], P('dp', ('tensor', 'vocab')), may hold values from -4 to 4
- draft_map: int32 [16384], P(('tensor', 'vocab')), may hold values from 0 to 98298, as said below
- drafted: int32 [1024], P('dp'), may hold values from 0 to 114681, as said below
Outputs:
- logprob: float32 [1024, 16384], P('dp', ('tensor', 'vocab'))
- drafted_logp: float32 [1024], P('dp')
Inputs may be any that keep to these rules, and one draw needn't show every extreme that they name: Draft id j stands for target id j + draft_map[j]; these target ids start at 0, rise strictly with j and stay below 128256. Every row's drafted id is the target id of exactly one draft id.
All inputs are finite; a program needn't handle non-finite values.
Results may differ from a plain program's by a relative error of at most 0.0029.
Values may be sent and summed in bfloat16 or wider, within the bound.
No kernel may reach another device: no remote copies, remote signals or barrier semaphores. Data moves between devices by JAX's collectives and lax.ppermute only.
A program may use at most 64 MiB of HBM per device.

v0:
```python
import jax
import jax.numpy as jnp
from jax import lax
from jax.sharding import PartitionSpec as P

D = 16384


eps = 1e-05


def body(features, fc_weight, norm_gain, head_weight, draft_map, drafted):
    all_rows = lax.all_gather(features, "dp", axis=0, tiled=True)
    partial_joined = jnp.dot(all_rows, fc_weight, preferred_element_type=jnp.float32)
    joined = lax.psum(partial_joined, ("tensor", "vocab"))
    square = lax.psum(jnp.sum(joined * joined, axis=1), "dp") / D
    normed = (joined * lax.rsqrt(square + eps)[:, None] * norm_gain[None, :]).astype(jnp.bfloat16)
    logits = lax.psum_scatter(
        jnp.dot(normed, head_weight, preferred_element_type=jnp.float32),
        "dp",
        scatter_dimension=0,
        tiled=True,
    )
    width = logits.shape[1]
    target = (
        draft_map + jnp.arange(width, dtype=jnp.int32) + lax.axis_index(("tensor", "vocab")) * width
    )
    hit = drafted[:, None] == target[None, :]
    own_pick = jnp.sum(jnp.where(hit, logits, jnp.float32(0.0)), axis=1)
    own_top = jnp.max(logits, axis=1)
    top = lax.pmax(own_top, ("tensor", "vocab"))
    own_total = jnp.sum(jnp.exp(logits - top[:, None]), axis=1)
    total, picked = lax.psum((own_total, own_pick), ("tensor", "vocab"))
    lse = top + jnp.log(total)
    return (logits - lse[:, None], picked - lse)


def solution(mesh):
    placed = (
        P("dp", ("tensor", "vocab")),
        P(("tensor", "vocab"), "dp"),
        P("dp"),
        P("dp", ("tensor", "vocab")),
        P(("tensor", "vocab")),
        P("dp"),
    )
    return jax.shard_map(
        body,
        mesh=mesh,
        in_specs=placed,
        out_specs=(P("dp", ("tensor", "vocab")), P("dp")),
        check_vma=False,
    )
```

profile of v0, /device:TPU:8, one launch (start us, length us, event | category | flops | bytes accessed | tf_op | source)
XLA Modules:
  0.0 484.1 jit_solution(10096191800505953681)
XLA Ops:
  7.2 0.0 copy-start
  7.2 0.0 all-gather.2.cloned.1.call-start
  7.2 0.7 all-gather.2.cloned.1.call-update
  7.9 0.0 all-reduce.3.cloned.1.call-start
  8.0 82.7 %all-gather.2.cloned.1.call-done = bf16[1024,1536]{1,0:T(8,128)(2,1)} async-done(((bf16[64,1536]{1,0:T(8,128)(2,1)}), bf16[1024,1536]{1,0:T(8,128)(2,1)}) %all-gather.2.cloned.1.call-update) | async-done | bytes 3145744 | tf_op jit(solution)/shard_map/all_gather | solution.py:13
  90.7 0.0 copy-done
  90.7 6.8 %fusion.4 = f32[1024,1024]{1,0:T(8,128)} fusion(bf16[1024,1536]{1,0:T(8,128)(2,1)} %all-gather.2.cloned.1.call-done, bf16[1536,1024]{1,0:T(8,128)(2,1)S(1)} %copy-done), kind=kOutput, calls=%fused_computation.12 | convolution fusion | flops 3221225472 | bytes 10485760 | tf_op jit(solution)/shard_map/dot_general | solution.py:14
  97.5 0.0 all-reduce.3.cloned.1.call-update
  97.5 0.0 copy-start.3
  97.5 0.0 reduce-scatter.2.cloned.1.call-start
  97.6 138.8 %all-reduce.3.cloned.1.call-done = f32[1024,1024]{1,0:T(8,128)} async-done(((f32[1024,1024]{1,0:T(8,128)}), f32[1024,1024]{1,0:T(8,128)}) %all-reduce.3.cloned.1.call-update) | async-done | bytes 4194320 | tf_op jit(solution)/shard_map/psum | solution.py:15
  236.4 2.5 multiply_reduce_fusion
  238.9 31.3 %psum.29 = f32[1024]{0:T(1024)S(1)} all-reduce(f32[1024]{0:T(1024)S(1)} %multiply_reduce_fusion), channel_id=1, replica_groups=mesh['dp'=16,'tensor'=8,'vocab'=4] {'dp'}, use_global_device_ids=true, to_apply=%region_2.0 | all-reduce | flops 1024 | bytes 8192 | tf_op jit(solution)/shard_map/psum | solution.py:16
  270.2 0.0 copy-done.3
  270.2 0.0 copy-start.1
  270.2 0.0 copy-start.2
  270.2 5.1 %fusion = f32[1024,512]{1,0:T(8,128)} fusion(bf16[1024,512]{1,0:T(8,128)(2,1)} %param.9, f32[1024,1024]{1,0:T(8,128)} %all-reduce.3.cloned.1.call-done, f32[1024]{0:T(1024)S(1)} %copy-done.3, f32[1024]{0:T(1024)S(1)} %add_rsqrt_fusion), kind=kOutput, calls=%fused_computation.2 | convolution fusion | flops 1076887552 | bytes 7348224 | tf_op jit(solution)/shard_map/dot_general | solution.py:19
  275.3 0.0 reduce-scatter.2.cloned.1.call-update
  275.4 0.0 copy-done.1
  275.4 70.2 %reduce-scatter.2.cloned.1.call-done = f32[64,512]{1,0:T(8,128)} async-done(((f32[1024,512]{1,0:T(8,128)}), f32[64,512]{1,0:T(8,128)}) %reduce-scatter.2.cloned.1.call-update) | async-done | bytes 131088 | tf_op jit(solution)/shard_map/reduce_scatter | solution.py:18
  345.6 1.0 reduce_max.9
  346.6 63.3 %pmax.7 = f32[64]{0:T(128)S(1)} all-reduce(f32[64]{0:T(128)S(1)} %reduce_max.9), channel_id=1, replica_groups=mesh['dp'=16,'tensor'=8,'vocab'=4] {'tensor','vocab'}, use_global_device_ids=true, to_apply=%region_5.6 | all-reduce | flops 64 | bytes 512 | tf_op jit(solution)/shard_map/pmax | solution.py:31
  409.9 0.0 copy-done.2
  409.9 1.1 select_reduce_fusion
  411.0 64.4 %all-reduce = (f32[64]{0:T(128)S(1)}, f32[64]{0:T(128)S(1)}) all-reduce(f32[64]{0:T(128)S(1)} %get-tuple-element.3, f32[64]{0:T(128)S(1)} %get-tuple-element.2), channel_id=1, replica_groups=mesh['dp'=16,'tensor'=8,'vocab'=4] {'tensor','vocab'}, use_global_device_ids=true, to_apply=%region_7.8 | all-reduce | flops 128 | bytes 1024 | tf_op jit(solution)/shard_map/psum | solution.py:33
  475.4 0.5 fusion.3
  475.9 1.6 broadcast_subtract_fusion
  (2 shorter events, 0.0 us)
Async XLA Ops:
  7.2 83.5 %copy-start = (bf16[1536,1024]{1,0:T(8,128)(2,1)S(1)}, bf16[1536,1024]{1,0:T(8,128)(2,1)}, u32[]{:S(2)}) copy-start(bf16[1536,1024]{1,0:T(8,128)(2,1)} %param.7) | copy-start | bytes 9437188
  7.2 83.5 %all-gather.2.cloned.1.call-start = ((), (), s32[]{:S(2)}) async-start(), calls=%async_computation.1 | async-start | bytes 3342336 | tf_op jit(solution)/shard_map/all_gather | solution.py:13
  7.9 228.5 %all-reduce.3.cloned.1.call-start = ((), (), s32[]{:S(2)}) async-start(), calls=%async_computation.2 | async-start | bytes 8388608 | tf_op jit(solution)/shard_map/psum | solution.py:15
  97.5 172.7 %copy-start.3 = (f32[1024]{0:T(1024)S(1)}, f32[1024]{0:T(1024)}, u32[]{:S(2)}) copy-start(f32[1024]{0:T(1024)} %param.8) | copy-start | bytes 12292
  97.5 248.1 %reduce-scatter.2.cloned.1.call-start = ((), (), s32[]{:S(2)}) async-start(), calls=%async_computation.3 | async-start | bytes 2228224 | tf_op jit(solution)/shard_map/reduce_scatter | solution.py:18
  270.2 5.2 %copy-start.1 = (s32[512]{0:T(512)S(1)}, s32[512]{0:T(512)}, u32[]{:S(2)}) copy-start(s32[512]{0:T(512)} %param.10) | copy-start | bytes 6148
  270.2 139.7 %copy-start.2 = (s32[64]{0:T(128)S(1)}, s32[64]{0:T(128)}, u32[]{:S(2)}) copy-start(s32[64]{0:T(128)} %param.11) | copy-start | bytes 772
Sparse Core Ops, SparseCore 0:
  10.1 80.5 all-gather.1
  97.6 138.6 all-reduce.2
  275.5 70.0 reduce-scatter.1
where the time goes:
time: 484 us
  waiting for transfers between devices  292 us (60%)
  blocking collectives  159 us (33%)
  between operations  13.8 us (3%)
  matrix products  12 us (2%)
  other arithmetic  6.82 us (1%)
    psum x1, waiting for transfers between devices, body(): joined = lax.psum(partial_joined, ('tensor', 'vocab'))  139 us
    all_gather x1, waiting for transfers between devices, body(): all_rows = lax.all_gather(features, 'dp', axis=0, tiled=True)  82.7 us
    reduce_scatter x1, waiting for transfers between devices, body(): lax.psum_scatter(jnp.dot(normed, head_weight, preferred_element_type=jnp....  70.2 us
    psum x1, blocking collectives, body(): total, picked = lax.psum((own_total, own_pick), ('tensor', 'vocab'))  64.4 us
    pmax x1, blocking collectives, body(): top = lax.pmax(own_top, ('tensor', 'vocab'))  63.3 us
    psum x1, blocking collectives, body(): square = lax.psum(jnp.sum(joined * joined, axis=1), 'dp') / D  31.3 us
  transfers between devices with their start and end apart: 3, of which 3 were waited for; matrix products, arithmetic and copies ran while one was open for 0% of the time, Pallas kernels for 0%

commit v1 on v0

v1 whole, which is shorter than its diff:
```python
import jax
import jax.numpy as jnp
from jax import lax
from jax.sharding import PartitionSpec as P

D = 16384
eps = 1e-05
PLANE = ("tensor", "vocab")
CHUNKS = 2


def scatter(a, axes, exchange):
    if not exchange:
        return lax.psum_scatter(a, axes, scatter_dimension=0, tiled=True)
    n = lax.axis_size(axes)
    got = lax.all_to_all(a, axes, 0, 0, tiled=True)
    return jnp.sum(got.reshape((n, got.shape[0] // n) + got.shape[1:]), axis=0)


def body(features, fc_weight, norm_gain, head_weight, draft_map, drafted):
    f32 = jnp.float32
    rows = features.shape[0] // CHUNKS
    shards = [
        lax.all_gather(features[c * rows : (c + 1) * rows], "dp", axis=0, tiled=True)
        for c in range(CHUNKS)
    ]
    logits, squares = [], []
    for c in range(CHUNKS):
        partial = jnp.dot(shards[c], fc_weight, preferred_element_type=f32)
        joined = scatter(partial, PLANE, c == 1)
        scaled = (joined * norm_gain).astype(jnp.bfloat16)
        scaled = lax.all_gather(scaled, PLANE, axis=0, tiled=True)
        squares.append(jnp.sum((scaled.astype(f32) / norm_gain) ** 2, axis=1))
        both = jnp.dot(scaled, head_weight, preferred_element_type=f32)
        logits.append(scatter(both, "dp", c == 1))
    logits = jnp.concatenate(logits)
    squares = [s.reshape(-1, rows) for s in squares]
    square = jnp.sum(lax.all_to_all(jnp.concatenate(squares, axis=1), "dp", 0, 0, tiled=True), axis=0) / D
    logits = logits * lax.rsqrt(square + eps)[:, None]

    width = logits.shape[1]
    target = draft_map + jnp.arange(width, dtype=jnp.int32) + lax.axis_index(PLANE) * width
    hit = drafted[:, None] == target[None, :]
    own_pick = jnp.sum(jnp.where(hit, logits, f32(0.0)), axis=1)
    own_top = jnp.max(logits, axis=1)
    own_total = jnp.sum(jnp.exp(logits - own_top[:, None]), axis=1)
    own = jnp.stack([own_top, own_total, own_pick])
    every = jnp.broadcast_to(own, (lax.axis_size(PLANE),) + own.shape)
    every = lax.all_to_all(every, PLANE, 0, 0, tiled=True)
    top = jnp.max(every[:, 0], axis=0)
    total = jnp.sum(every[:, 1] * jnp.exp(every[:, 0] - top), axis=0)
    picked = jnp.sum(every[:, 2], axis=0)
    lse = top + jnp.log(total)
    return (logits - lse[:, None], picked - lse)


def solution(mesh):
    placed = (
        P("dp", ("tensor", "vocab")),
        P(("tensor", "vocab"), "dp"),
        P("dp"),
        P("dp", ("tensor", "vocab")),
        P(("tensor", "vocab")),
        P("dp"),
    )
    return jax.shard_map(
        body,
        mesh=mesh,
        in_specs=placed,
        out_specs=(P("dp", ("tensor", "vocab")), P("dp")),
        check_vma=False,
    )
```

time: 484 us -> 531 us (1.097)
  the two profiles are of different devices: /device:TPU:8 before, /device:TPU:1 now
where the time goes in v1:
time: 531 us; the launch traced here: 530 us
  waiting for transfers between devices  402 us (76%)
  blocking collectives  67.7 us (13%)
  starting transfers between devices  16.6 us (3%)
  matrix products  14.3 us (3%)
  between operations  14.2 us (3%)
  other arithmetic  12.4 us (2%)
    all_gather x2, waiting for transfers between devices, body(): lax.all_gather(features[c * rows:(c + 1) * rows], 'dp', axis=0, tiled=True)  136 us
    all_gather x2, waiting for transfers between devices, body(): scaled = lax.all_gather(scaled, PLANE, axis=0, tiled=True)  122 us
    reduce_scatter x2, waiting for transfers between devices, scatter(): return lax.psum_scatter(a, axes, scatter_dimension=0, tiled=True)  91.1 us
    all_to_all x1, waiting for transfers between devices, scatter(): got = lax.all_to_all(a, axes, 0, 0, tiled=True)  44.6 us
    all_to_all x1, blocking collectives, scatter(): got = lax.all_to_all(a, axes, 0, 0, tiled=True)  44.6 us
    all_to_all x1, blocking collectives, body(): every = lax.all_to_all(every, PLANE, 0, 0, tiled=True)  23.1 us
    all_to_all x1, starting transfers between devices, body(): lax.all_to_all(jnp.concatenate(squares, axis=1), 'dp', 0, 0, tiled=True)  12 us
  transfers between devices with their start and end apart: 8, of which 8 were waited for; matrix products, arithmetic and copies ran while one was open for 3% of the time, Pallas kernels for 0%

profile of v1, /device:TPU:1, one launch (start us, length us, event | category | flops | bytes accessed | tf_op | source)
XLA Modules:
  0.0 530.2 jit_solution(6812820860162823203)
XLA Ops:
  7.2 1.8 fusion.2
  9.1 0.7 all-gather.9.cloned.1.call-update
  9.8 68.2 %all-gather.5.cloned.1.call-done = bf16[512,1536]{1,0:T(8,128)(2,1)} async-done(((bf16[32,1536]{1,0:T(8,128)(2,1)}), bf16[512,1536]{1,0:T(8,128)(2,1)}) %all-gather.5.cloned.1.call-update) | async-done | bytes 1572880 | tf_op jit(solution)/shard_map/all_gather | solution.py:24
  78.0 4.5 fusion.4
  82.7 67.3 %all-gather.9.cloned.1.call-done = bf16[512,1536]{1,0:T(8,128)(2,1)} async-done(((bf16[32,1536]{1,0:T(8,128)(2,1)}), bf16[512,1536]{1,0:T(8,128)(2,1)}) %all-gather.9.cloned.1.call-update) | async-done | bytes 1572880 | tf_op jit(solution)/shard_map/all_gather | solution.py:24
  150.0 3.2 fusion.6
  153.2 44.6 %all_to_all.32 = f32[32,16,1024]{2,1,0:T(8,128)} all-to-all(f32[32,16,1024]{2,1,0:T(8,128)S(1)} %bitcast.19), channel_id=1, replica_groups=mesh['dp'=16,'tensor'=8,'vocab'=4] {'tensor','vocab'}, dimensions={0} | all-to-all | bytes 4194304 | tf_op jit(solution)/shard_map/all_to_all | solution.py:16
  197.8 1.8 reduce_sum.81
  199.6 61.8 %reduce-scatter.3.cloned.1.call-done = f32[16,1024]{1,0:T(8,128)} async-done(((f32[512,1024]{1,0:T(8,128)}), f32[16,1024]{1,0:T(8,128)}) %reduce-scatter.3.cloned.1.call-update) | async-done | bytes 65552 | tf_op jit(solution)/shard_map/reduce_scatter | solution.py:14
  261.4 1.5 multiply_convert_fusion
  263.0 0.5 all-gather.7.cloned.1.call-update
  263.5 61.1 %all-gather.11.cloned.1.call-done = bf16[512,1024]{1,0:T(8,128)(2,1)} async-done(((bf16[16,1024]{1,0:T(8,128)(2,1)}), bf16[512,1024]{1,0:T(8,128)(2,1)}) %all-gather.11.cloned.1.call-update) | async-done | bytes 1048592 | tf_op jit(solution)/shard_map/all_gather | solution.py:32
  324.6 60.6 %all-gather.7.cloned.1.call-done = bf16[512,1024]{1,0:T(8,128)(2,1)} async-done(((bf16[16,1024]{1,0:T(8,128)(2,1)}), bf16[512,1024]{1,0:T(8,128)(2,1)}) %all-gather.7.cloned.1.call-update) | async-done | bytes 1048592 | tf_op jit(solution)/shard_map/all_gather | solution.py:32
  385.2 2.2 multiply_reduce_fusion.1
  387.5 0.7 pad_maximum_fusion
  388.2 12.0 %all-to-all-start.2 = ((f32[16,1,64]{2,1,0:T(1,128)}), f32[16,1,64]{2,1,0:T(1,128)S(1)}, u32[]{:S(2)}, u32[]{:S(2)}) async-start(f32[16,1,64]{2,1,0:T(1,128)} %bitcast.2), calls=%async_computation.4 | async-start | bytes 16384 | tf_op jit(solution)/shard_map/all_to_all | solution.py:38
  400.2 3.3 fusion.7
  403.5 8.0 %all-to-all-done.2 = f32[16,1,64]{2,1,0:T(1,128)S(1)} async-done(((f32[16,1,64]{2,1,0:T(1,128)}), f32[16,1,64]{2,1,0:T(1,128)S(1)}, u32[]{:S(2)}, u32[]{:S(2)}) %all-to-all-start.2) | async-done | bytes 4128 | tf_op jit(solution)/shard_map/all_to_all | solution.py:38
  411.5 4.3 all-to-all-start.1
  415.9 3.2 fusion.5
  419.2 44.6 %all-to-all-done.1 = f32[16,32,512]{2,1,0:T(8,128)} async-done(((f32[16,32,512]{2,1,0:T(8,128)}), f32[16,32,512]{2,1,0:T(8,128)}, u32[]{:S(2)}, u32[]{:S(2)}) %all-to-all-start.1) | async-done | bytes 1048608 | tf_op jit(solution)/shard_map/all_to_all | solution.py:16
  463.9 1.3 reduce_sum.82
  465.2 29.3 %reduce-scatter.5.cloned.1.call-done = f32[32,512]{1,0:T(8,128)} async-done(((f32[512,512]{1,0:T(8,128)}), f32[32,512]{1,0:T(8,128)}) %reduce-scatter.5.cloned.1.call-update) | async-done | bytes 65552 | tf_op jit(solution)/shard_map/reduce_scatter | solution.py:14
  494.4 1.0 fusion
  495.5 1.0 exponential_reduce_fusion
  496.6 0.1 reshape.38
  496.7 23.1 %all_to_all.33 = f32[32,1,192]{2,1,0:T(1,128)S(1)} all-to-all(f32[32,1,192]{2,1,0:T(1,128)S(1)} %reshape.38), channel_id=1, replica_groups=mesh['dp'=16,'tensor'=8,'vocab'=4] {'tensor','vocab'}, dimensions={0} | all-to-all | bytes 49152 | tf_op jit(solution)/shard_map/all_to_all | solution.py:49
  519.8 0.5 broadcast.14
  520.3 0.7 reduce.5
  521.0 0.1 reshape.39
  521.2 0.5 fusion.1
  521.7 1.6 broadcast_subtract_fusion
  (29 shorter events, 0.7 us)
Async XLA Ops:
  7.2 70.9 %copy-start = (bf16[1536,1024]{1,0:T(8,128)(2,1)S(1)}, bf16[1536,1024]{1,0:T(8,128)(2,1)}, u32[]{:S(2)}) copy-start(bf16[1536,1024]{1,0:T(8,128)(2,1)} %param.7) | copy-start | bytes 9437188
  7.2 70.9 %all-gather.5.cloned.1.call-start = ((), (), s32[]{:S(2)}) async-start(), calls=%async_computation.6 | async-start | bytes 1671168 | tf_op jit(solution)/shard_map/all_gather | solution.py:24
  9.0 141.0 %all-gather.9.cloned.1.call-start = ((), (), s32[]{:S(2)}) async-start(), calls=%async_computation.10 | async-start | bytes 1671168 | tf_op jit(solution)/shard_map/all_gather | solution.py:24
  9.8 251.7 %reduce-scatter.3.cloned.1.call-start = ((), (), s32[]{:S(2)}) async-start(), calls=%async_computation.7 | async-start | bytes 2162688 | tf_op jit(solution)/shard_map/reduce_scatter | solution.py:14
  82.6 242.0 %all-gather.11.cloned.1.call-start = ((), (), s32[]{:S(2)}) async-start(), calls=%async_computation.11 | async-start | bytes 1081344 | tf_op jit(solution)/shard_map/all_gather | solution.py:32
  197.8 63.6 %copy-start.1 = (f32[1024]{0:T(1024)S(1)}, f32[1024]{0:T(1024)}, u32[]{:S(2)}) copy-start(f32[1024]{0:T(1024)} %param.8) | copy-start | bytes 12292
  262.9 122.3 %all-gather.7.cloned.1.call-start = ((), (), s32[]{:S(2)}) async-start(), calls=%async_computation.8 | async-start | bytes 1081344 | tf_op jit(solution)/shard_map/all_gather | solution.py:32
  388.2 23.3 %all-to-all-start.2 = ((f32[16,1,64]{2,1,0:T(1,128)}), f32[16,1,64]{2,1,0:T(1,128)S(1)}, u32[]{:S(2)}, u32[]{:S(2)}) async-start(f32[16,1,64]{2,1,0:T(1,128)} %bitcast.2), calls=%async_computation.4 | async-start | bytes 16384 | tf_op jit(solution)/shard_map/all_to_all | solution.py:38
  411.5 52.4 %all-to-all-start.1 = ((f32[16,32,512]{2,1,0:T(8,128)}), f32[16,32,512]{2,1,0:T(8,128)}, u32[]{:S(2)}, u32[]{:S(2)}) async-start(f32[16,32,512]{2,1,0:T(8,128)} %bitcast.20), calls=%async_computation.3 | async-start | bytes 2097152 | tf_op jit(solution)/shard_map/all_to_all | solution.py:16
  415.8 3.3 copy-start.2
  415.8 79.6 %copy-start.3 = (s32[64]{0:T(128)S(1)}, s32[64]{0:T(128)}, u32[]{:S(2)}) copy-start(s32[64]{0:T(128)} %param.11) | copy-start | bytes 772
  415.8 78.6 %reduce-scatter.5.cloned.1.call-start = ((), (), s32[]{:S(2)}) async-start(), calls=%async_computation.9 | async-start | bytes 1114112 | tf_op jit(solution)/shard_map/reduce_scatter | solution.py:14
Sparse Core Ops, SparseCore 0:
  10.1 67.9 all-gather.4
  80.7 69.2 all-gather.8
  154.4 106.9 reduce-scatter.2
  265.0 59.5 all-gather.10
  327.6 57.5 all-gather.6
  419.3 75.1 reduce-scatter.4

commit v2 on v1

v2 whole, which is shorter than its diff:
```python
import jax
import jax.numpy as jnp
from jax import lax
from jax.sharding import PartitionSpec as P

eps = 1e-05
PLANE = ("tensor", "vocab")
CHUNKS = 2
f16, bf16, f32 = jnp.float16, jnp.bfloat16, jnp.float32

UP = 2.0**9
PARTIAL = 2.0**-2
SCALED = 2.0**-7

CORE_PAIRS = [(i, i ^ 1) for i in range(8)]
SAME_CORE = [[(2 * x + c) * 4 + y for x in range(4) for y in range(4)] for c in range(2)]
PEERS = 16


def exchange(a):
    return lax.all_to_all(a, PLANE, 0, 0, axis_index_groups=SAME_CORE)


def after(a, b):
    return a if b is None else lax.optimization_barrier((a, b))[0]


def body(features, fc_weight, norm_gain, head_weight, draft_map, drafted):
    core = lax.axis_index("tensor") % 2
    z = lax.axis_size("dp")
    sent = (features.astype(f32) * UP).astype(f16)
    every = lax.all_gather(sent, "dp")
    depth = fc_weight.shape[1]
    rows = features.shape[0]
    part = rows // CHUNKS

    def joined_part(first):
        block = lax.dynamic_slice_in_dim(every, first, z // 2, 0).astype(bf16)
        return jnp.dot(block, fc_weight, preferred_element_type=f32) * (PARTIAL / UP)

    away = joined_part((1 - core) * (z // 2)).astype(f16)
    away = lax.ppermute(away, "tensor", CORE_PAIRS)
    chip = (joined_part(core * (z // 2)) + away.astype(f32)).astype(f16)

    logits, squares, sent, both = [], [], None, None
    for c in range(CHUNKS):
        mine = chip[:, c * part : (c + 1) * part].reshape(PEERS, -1, depth)
        got = after(exchange(mine), sent)
        joined = jnp.sum(got.astype(f32), axis=0)
        scaled = (joined * (norm_gain * (SCALED / PARTIAL))).astype(f16)
        sent = jnp.broadcast_to(scaled, (PEERS,) + scaled.shape)
        scaled = after(exchange(sent).reshape(-1, depth), both)
        other = lax.ppermute(scaled, "tensor", CORE_PAIRS)
        scaled = jnp.where(
            core == 0, jnp.concatenate([scaled, other]), jnp.concatenate([other, scaled])
        )
        own = scaled.astype(f32) * (1.0 / (norm_gain * SCALED))
        square = jnp.mean(own * own, axis=1) + eps
        both = jnp.dot(scaled.astype(bf16), head_weight, preferred_element_type=f32)
        both = (both * (lax.rsqrt(square) / SCALED)[:, None]).astype(f16)
        squares.append(square.reshape(z, part))
        logits.append(lax.all_to_all(both.reshape(z, part, -1), "dp", 0, 0))

    square = lax.all_to_all(jnp.concatenate(squares, axis=1), "dp", 0, 0)
    back = jnp.sqrt(square / jnp.mean(square, axis=0))
    logits = [
        jnp.sum(got.astype(f32) * back[:, c * part : (c + 1) * part, None], axis=0)
        for c, got in enumerate(logits)
    ]
    logits = jnp.concatenate(logits)

    width = logits.shape[1]
    target = draft_map + jnp.arange(width, dtype=jnp.int32) + lax.axis_index(PLANE) * width
    hit = drafted[:, None] == target[None, :]
    own_pick = jnp.sum(jnp.where(hit, logits, f32(0.0)), axis=1)
    own_top = jnp.max(logits, axis=1)
    own_total = jnp.sum(jnp.exp(logits - own_top[:, None]), axis=1)
    own = jnp.pad(jnp.stack([own_top, own_total, own_pick]), ((0, 5), (0, 128 - rows)))
    every = lax.all_to_all(jnp.broadcast_to(own, (lax.axis_size(PLANE),) + own.shape), PLANE, 0, 0)
    every = every[:, :, :rows]
    top = jnp.max(every[:, 0], axis=0)
    total = jnp.sum(every[:, 1] * jnp.exp(every[:, 0] - top), axis=0)
    picked = jnp.sum(every[:, 2], axis=0)
    lse = top + jnp.log(total)
    return (logits - lse[:, None], picked - lse)


def solution(mesh):
    placed = (
        P("dp", ("tensor", "vocab")),
        P(("tensor", "vocab"), "dp"),
        P("dp"),
        P("dp", ("tensor", "vocab")),
        P(("tensor", "vocab")),
        P("dp"),
    )
    return jax.shard_map(
        body,
        mesh=mesh,
        in_specs=placed,
        out_specs=(P("dp", ("tensor", "vocab")), P("dp")),
        check_vma=False,
    )
```

time: 531 us -> 251 us (0.47)
  waiting for transfers between devices: 402 us -> 62.4 us
  starting transfers between devices: 16.6 us -> 54.2 us
  blocking collectives: 67.7 us -> 103 us
  between operations: 14.2 us -> 0.88 us
    all_gather x4 -> x0, waiting for transfers between devices: 257 us -> none  [the longest x2 136 us: body(): lax.all_gather(features[c * rows:(c + 1) * rows], 'dp', axis=0, tiled=True)]
    reduce_scatter x2 -> x0, waiting for transfers between devices: 91.1 us -> none  [scatter(): return lax.psum_scatter(a, axes, scatter_dimension=0, tiled=True)]
    all_gather x0 -> x1, blocking collectives: none -> 54.8 us  [body(): every = lax.all_gather(sent, 'dp')]
    ppermute x0 -> x3, starting transfers between devices: none -> 22.2 us  [the longest x2 12.6 us: body(): other = lax.ppermute(scaled, 'tensor', CORE_PAIRS)]
    all_to_all x2 -> x3, blocking collectives: 67.7 us -> 48.7 us  [the longest x1 18 us: body(): square = lax.all_to_all(jnp.concatenate(squares, axis=1), 'dp', 0, 0)]
    all_to_all x2 -> x5, starting transfers between devices: 16.3 us -> 31.9 us  [the longest x2 16.7 us: body(): logits.append(lax.all_to_all(both.reshape(z, part, -1), 'dp', 0, 0))]
    all_to_all x2 -> x5, waiting for transfers between devices: 52.6 us -> 58.1 us  [the longest x2 40.7 us: body(): logits.append(lax.all_to_all(both.reshape(z, part, -1), 'dp', 0, 0))]
  transfers between devices with their start and end apart: 8 -> 8, of which waited for: 8 -> 7; matrix products, arithmetic and copies ran while one was open for 3% -> 5% of each run, Pallas kernels for 0% -> 0%
where the time goes in v2:
time: 251 us; the launch traced here: 250 us
  blocking collectives  103 us (41%)
  waiting for transfers between devices  62.4 us (25%)
  starting transfers between devices  54.2 us (22%)
  matrix products  14.6 us (6%)
  other arithmetic  12 us (5%)
    all_gather x1, blocking collectives, body(): every = lax.all_gather(sent, 'dp')  54.8 us
    all_to_all x2, waiting for transfers between devices, body(): logits.append(lax.all_to_all(both.reshape(z, part, -1), 'dp', 0, 0))  40.7 us
    all_to_all x1, blocking collectives, body(): square = lax.all_to_all(jnp.concatenate(squares, axis=1), 'dp', 0, 0)  18 us
    all_to_all x1, blocking collectives, body(): lax.all_to_all(jnp.broadcast_to(own, (lax.axis_size(PLANE),) + own.shape)...  17.8 us
    all_to_all x3, waiting for transfers between devices, exchange(): return lax.all_to_all(a, PLANE, 0, 0, axis_index_groups=SAME_CORE)  17.4 us
    all_to_all x2, starting transfers between devices, body(): logits.append(lax.all_to_all(both.reshape(z, part, -1), 'dp', 0, 0))  16.7 us
    all_to_all x3, starting transfers between devices, exchange(): return lax.all_to_all(a, PLANE, 0, 0, axis_index_groups=SAME_CORE)  15.3 us
    all_to_all x1, blocking collectives, exchange(): return lax.all_to_all(a, PLANE, 0, 0, axis_index_groups=SAME_CORE)  12.8 us
  transfers between devices with their start and end apart: 8, of which 7 were waited for; matrix products, arithmetic and copies ran while one was open for 5% of the time, Pallas kernels for 0%

profile of v2, /device:TPU:1, one launch (start us, length us, event | category | flops | bytes accessed | tf_op | source)
XLA Modules:
  0.0 250.0 jit_solution(4362268849934494926)
XLA Ops:
  0.7 1.1 multiply_convert_fusion.1
  1.8 54.8 %all-gather.2 = f16[1024,1536]{1,0:T(8,128)(2,1)} all-gather(f16[64,1536]{1,0:T(8,128)(2,1)S(1)} %multiply_convert_fusion.1), channel_id=2, replica_groups=mesh['dp'=16,'tensor'=8,'vocab'=4] {'dp'}, dimensions={0}, use_global_device_ids=true | all-gather | bytes 3342336 | tf_op jit(solution)/shard_map/all_gather | solution.py:32
  56.6 4.2 %multiply_convert_fusion = f16[8,64,1024]{2,1,0:T(8,128)(2,1)} fusion(bf16[1536,1024]{1,0:T(8,128)(2,1)S(1)} %copy-done, f16[16,64,1536]{2,1,0:T(8,128)(2,1)} %bitcast.28, s32[]{:T(128)S(6)} %select_n.32), kind=kOutput, calls=%fused_computation.7 | convolution fusion | flops 1612447744 | bytes 5767172 | tf_op jit(solution)/shard_map/dot_general | solution.py:39
  60.8 9.7 %collective-permute-start = (f16[8,64,1024]{2,1,0:T(8,128)(2,1)}, f16[8,64,1024]{2,1,0:T(8,128)(2,1)}, u32[]{:S(2)}, u32[]{:S(2)}) collective-permute-start(f16[8,64,1024]{2,1,0:T(8,128)(2,1)} %multiply_convert_fusion), channel_id=1, source_target_pairs={{0,4},{4,0},{8,12},{12,8},{16,20},{20,16},{24,28},{28,24},{1,5},{5... | collective-permute-start | bytes 3145736 | tf_op jit(solution)/shard_map/ppermute | solution.py:42
  70.5 2.6 %collective-permute-done = f16[8,64,1024]{2,1,0:T(8,128)(2,1)} collective-permute-done((f16[8,64,1024]{2,1,0:T(8,128)(2,1)}, f16[8,64,1024]{2,1,0:T(8,128)(2,1)}, u32[]{:S(2)}, u32[]{:S(2)}) %collective-permute-start) | collective-permute-done | bytes 1048608 | tf_op jit(solution)/shard_map/ppermute | solution.py:42
  73.0 3.5 %add_convert_fusion = f16[8,64,1024]{2,1,0:T(8,128)(2,1)S(1)} fusion(f16[8,64,1024]{2,1,0:T(8,128)(2,1)} %collective-permute-done, bf16[1536,1024]{1,0:T(8,128)(2,1)S(1)} %copy-done, f16[16,64,1536]{2,1,0:T(8,128)(2,1)} %bitcast.29, s32[]{:T(128)S(6)} %select_n.31), kind=kOutput, calls=%fused_computation.6 | convolution fusion | flops 1613496320 | bytes 6815748 | tf_op jit(solution)/shard_map/dot_general | solution.py:39
  76.6 1.3 fusion.22
  77.9 6.8 %all-to-all-start = ((f16[16,16,1024]{2,1,0:T(8,128)(2,1)}), f16[16,16,1024]{2,1,0:T(8,128)(2,1)}, u32[]{:S(2)}, u32[]{:S(2)}) async-start(f16[16,16,1024]{2,1,0:T(8,128)(2,1)} %bitcast.34), calls=%async_computation | async-start | bytes 1048576 | tf_op jit(solution)/shard_map/all_to_all | solution.py:21
  84.7 10.4 %all-to-all-done = f16[16,16,1024]{2,1,0:T(8,128)(2,1)} async-done(((f16[16,16,1024]{2,1,0:T(8,128)(2,1)}), f16[16,16,1024]{2,1,0:T(8,128)(2,1)}, u32[]{:S(2)}, u32[]{:S(2)}) %all-to-all-start) | async-done | bytes 524320 | tf_op jit(solution)/shard_map/all_to_all | solution.py:21
  95.1 1.1 convert_reduce_fusion.1
  96.3 12.8 %all_to_all.47 = f16[16,16,1024]{2,1,0:T(8,128)(2,1)} all-to-all(f16[16,16,1024]{2,1,0:T(8,128)(2,1)S(1)} %broadcast_in_dim.9), channel_id=1, replica_groups={{0,1,2,3,8,9,10,11,16,17,18,19,24,25,26,27},{4,5,6,7,12,13,14,15,20,21,..., dimensions={0} | all-to-all | bytes 1048576 | tf_op jit(solution)/shard_map/all_to_all | solution.py:21
  109.1 4.2 %all-to-all-start.3 = ((f16[16,16,1024]{2,1,0:T(8,128)(2,1)}), f16[16,16,1024]{2,1,0:T(8,128)(2,1)}, u32[]{:S(2)}, u32[]{:S(2)}) async-start(f16[16,16,1024]{2,1,0:T(8,128)(2,1)} %bitcast.33), calls=%async_computation.3 | async-start | bytes 1048576 | tf_op jit(solution)/shard_map/all_to_all | solution.py:21
  113.4 5.2 %collective-permute-start.1 = (f16[256,1024]{1,0:T(8,128)(2,1)}, f16[256,1024]{1,0:T(8,128)(2,1)}, u32[]{:S(2)}, u32[]{:S(2)}) collective-permute-start(f16[256,1024]{1,0:T(8,128)(2,1)} %bitcast.30), channel_id=1, source_target_pairs={{0,4},{4,0},{8,12},{12,8},{16,20},{20,16},{24,28},{28,24},{1,5},{5... | collective-permute-start | bytes 1572872 | tf_op jit(solution)/shard_map/ppermute | solution.py:53
  118.5 3.8 %all-to-all-done.3 = f16[16,16,1024]{2,1,0:T(8,128)(2,1)} async-done(((f16[16,16,1024]{2,1,0:T(8,128)(2,1)}), f16[16,16,1024]{2,1,0:T(8,128)(2,1)}, u32[]{:S(2)}, u32[]{:S(2)}) %all-to-all-start.3) | async-done | bytes 524320 | tf_op jit(solution)/shard_map/all_to_all | solution.py:21
  122.3 1.1 convert_reduce_fusion
  123.5 0.9 broadcast_in_dim.10
  124.3 4.2 %all-to-all-start.4 = ((f16[16,16,1024]{2,1,0:T(8,128)(2,1)}), f16[16,16,1024]{2,1,0:T(8,128)(2,1)}, u32[]{:S(2)}, u32[]{:S(2)}) async-start(f16[16,16,1024]{2,1,0:T(8,128)(2,1)} %broadcast_in_dim.10), calls=%async_computation.4 | async-start | bytes 1048576 | tf_op jit(solution)/shard_map/all_to_all | solution.py:21
  128.6 2.2 multiply_reduce_fusion.1
  130.8 3.5 %fusion.12 = f16[512,512]{1,0:T(8,128)(2,1)} fusion(bf16[1024,512]{1,0:T(8,128)(2,1)} %param.9, f32[512]{0:T(512)S(1)} %get-tuple-element.20, f16[256,1024]{1,0:T(8,128)(2,1)} %collective-permute-done.1, f16[256,1024]{1,0:T(8,128)(2,1)} %bitcast.32, pred[]{:T(512)S(6)} %eq.10), kind=kOutput, calls=%fused_computation.14 | convolution fusion | flops 539492352 | bytes 2623489 | tf_op jit(solution)/shard_map/dot_general | solution.py:59
  134.3 3.2 %all-to-all-done.4 = f16[16,16,1024]{2,1,0:T(8,128)(2,1)} async-done(((f16[16,16,1024]{2,1,0:T(8,128)(2,1)}), f16[16,16,1024]{2,1,0:T(8,128)(2,1)}, u32[]{:S(2)}, u32[]{:S(2)}) %all-to-all-start.4) | async-done | bytes 524320 | tf_op jit(solution)/shard_map/all_to_all | solution.py:21
  137.5 7.4 %collective-permute-start.2 = (f16[256,1024]{1,0:T(8,128)(2,1)}, f16[256,1024]{1,0:T(8,128)(2,1)}, u32[]{:S(2)}, u32[]{:S(2)}) collective-permute-start(f16[256,1024]{1,0:T(8,128)(2,1)} %bitcast.6), channel_id=1, source_target_pairs={{0,4},{4,0},{8,12},{12,8},{16,20},{20,16},{24,28},{28,24},{1,5},{5... | collective-permute-start | bytes 1572872 | tf_op jit(solution)/shard_map/ppermute | solution.py:53
  145.1 1.8 collective-permute-done.2
  146.8 2.1 multiply_reduce_fusion
  149.1 18.0 %all_to_all.48 = f32[16,1,64]{2,1,0:T(1,128)S(1)} all-to-all(f32[16,1,64]{2,1,0:T(1,128)S(1)} %bitcast.42), channel_id=1, replica_groups=mesh['dp'=16,'tensor'=8,'vocab'=4] {'dp'}, dimensions={0} | all-to-all | bytes 8192 | tf_op jit(solution)/shard_map/all_to_all | solution.py:64
  167.1 4.2 %all-to-all-start.2 = ((f16[16,32,512]{2,1,0:T(8,128)(2,1)}), f16[16,32,512]{2,1,0:T(8,128)(2,1)}, u32[]{:S(2)}, u32[]{:S(2)}) async-start(f16[16,32,512]{2,1,0:T(8,128)(2,1)} %bitcast.36), calls=%async_computation.2 | async-start | bytes 1048576 | tf_op jit(solution)/shard_map/all_to_all | solution.py:62
  171.4 3.4 %fusion.13 = f16[512,512]{1,0:T(8,128)(2,1)} fusion(bf16[1024,512]{1,0:T(8,128)(2,1)} %param.9, f32[512]{0:T(512)S(1)} %get-tuple-element.22, f16[256,1024]{1,0:T(8,128)(2,1)} %collective-permute-done.2, f16[256,1024]{1,0:T(8,128)(2,1)} %bitcast.6, pred[]{:T(512)S(6)} %eq.10), kind=kOutput, calls=%fused_computation.15 | convolution fusion | flops 539492352 | bytes 2623489 | tf_op jit(solution)/shard_map/dot_general | solution.py:59
  174.8 19.2 %all-to-all-done.2 = f16[16,32,512]{2,1,0:T(8,128)(2,1)} async-done(((f16[16,32,512]{2,1,0:T(8,128)(2,1)}), f16[16,32,512]{2,1,0:T(8,128)(2,1)}, u32[]{:S(2)}, u32[]{:S(2)}) %all-to-all-start.2) | async-done | bytes 524320 | tf_op jit(solution)/shard_map/all_to_all | solution.py:62
  194.0 12.4 %all-to-all-start.6 = ((f16[16,32,512]{2,1,0:T(8,128)(2,1)}), f16[16,32,512]{2,1,0:T(8,128)(2,1)}, u32[]{:S(2)}, u32[]{:S(2)}) async-start(f16[16,32,512]{2,1,0:T(8,128)(2,1)} %bitcast.35), calls=%async_computation.6 | async-start | bytes 1048576 | tf_op jit(solution)/shard_map/all_to_all | solution.py:62
  206.6 1.2 multiply_reduce_fusion.3
  207.8 21.5 %all-to-all-done.6 = f16[16,32,512]{2,1,0:T(8,128)(2,1)} async-done(((f16[16,32,512]{2,1,0:T(8,128)(2,1)}), f16[16,32,512]{2,1,0:T(8,128)(2,1)}, u32[]{:S(2)}, u32[]{:S(2)}) %all-to-all-start.6) | async-done | bytes 524320 | tf_op jit(solution)/shard_map/all_to_all | solution.py:62
  229.3 1.2 multiply_reduce_fusion.2
  230.8 17.8 %all_to_all.49 = f32[32,8,128]{2,1,0:T(8,128)S(1)} all-to-all(f32[32,8,128]{2,1,0:T(8,128)S(1)} %broadcast_in_dim.12), channel_id=1, replica_groups=mesh['dp'=16,'tensor'=8,'vocab'=4] {'tensor','vocab'}, dimensions={0} | all-to-all | bytes 262144 | tf_op jit(solution)/shard_map/all_to_all | solution.py:79
  (33 shorter events, 2.2 us)
Async XLA Ops:
  0.6 56.0 %copy-start = (bf16[1536,1024]{1,0:T(8,128)(2,1)S(1)}, bf16[1536,1024]{1,0:T(8,128)(2,1)}, u32[]{:S(2)}) copy-start(bf16[1536,1024]{1,0:T(8,128)(2,1)} %param.7) | copy-start | bytes 9437188
  60.8 12.3 %collective-permute-start = (f16[8,64,1024]{2,1,0:T(8,128)(2,1)}, f16[8,64,1024]{2,1,0:T(8,128)(2,1)}, u32[]{:S(2)}, u32[]{:S(2)}) collective-permute-start(f16[8,64,1024]{2,1,0:T(8,128)(2,1)} %multiply_convert_fusion), channel_id=1, source_target_pairs={{0,4},{4,0},{8,12},{12,8},{16,20},{20,16},{24,28},{28,24},{1,5},{5... | collective-permute-start | bytes 3145736 | tf_op jit(solution)/shard_map/ppermute | solution.py:42
  76.6 8.1 %copy-start.1 = (f32[1024]{0:T(1024)S(1)}, f32[1024]{0:T(1024)}, u32[]{:S(2)}) copy-start(f32[1024]{0:T(1024)} %param.8) | copy-start | bytes 12292
  77.9 17.2 %all-to-all-start = ((f16[16,16,1024]{2,1,0:T(8,128)(2,1)}), f16[16,16,1024]{2,1,0:T(8,128)(2,1)}, u32[]{:S(2)}, u32[]{:S(2)}) async-start(f16[16,16,1024]{2,1,0:T(8,128)(2,1)} %bitcast.34), calls=%async_computation | async-start | bytes 1048576 | tf_op jit(solution)/shard_map/all_to_all | solution.py:21
  109.1 13.2 %all-to-all-start.3 = ((f16[16,16,1024]{2,1,0:T(8,128)(2,1)}), f16[16,16,1024]{2,1,0:T(8,128)(2,1)}, u32[]{:S(2)}, u32[]{:S(2)}) async-start(f16[16,16,1024]{2,1,0:T(8,128)(2,1)} %bitcast.33), calls=%async_computation.3 | async-start | bytes 1048576 | tf_op jit(solution)/shard_map/all_to_all | solution.py:21
  113.4 15.2 %collective-permute-start.1 = (f16[256,1024]{1,0:T(8,128)(2,1)}, f16[256,1024]{1,0:T(8,128)(2,1)}, u32[]{:S(2)}, u32[]{:S(2)}) collective-permute-start(f16[256,1024]{1,0:T(8,128)(2,1)} %bitcast.30), channel_id=1, source_target_pairs={{0,4},{4,0},{8,12},{12,8},{16,20},{20,16},{24,28},{28,24},{1,5},{5... | collective-permute-start | bytes 1572872 | tf_op jit(solution)/shard_map/ppermute | solution.py:53
  124.3 13.2 %all-to-all-start.4 = ((f16[16,16,1024]{2,1,0:T(8,128)(2,1)}), f16[16,16,1024]{2,1,0:T(8,128)(2,1)}, u32[]{:S(2)}, u32[]{:S(2)}) async-start(f16[16,16,1024]{2,1,0:T(8,128)(2,1)} %broadcast_in_dim.10), calls=%async_computation.4 | async-start | bytes 1048576 | tf_op jit(solution)/shard_map/all_to_all | solution.py:21
  137.5 9.3 %collective-permute-start.2 = (f16[256,1024]{1,0:T(8,128)(2,1)}, f16[256,1024]{1,0:T(8,128)(2,1)}, u32[]{:S(2)}, u32[]{:S(2)}) collective-permute-start(f16[256,1024]{1,0:T(8,128)(2,1)} %bitcast.6), channel_id=1, source_target_pairs={{0,4},{4,0},{8,12},{12,8},{16,20},{20,16},{24,28},{28,24},{1,5},{5... | collective-permute-start | bytes 1572872 | tf_op jit(solution)/shard_map/ppermute | solution.py:53
  167.1 26.9 %all-to-all-start.2 = ((f16[16,32,512]{2,1,0:T(8,128)(2,1)}), f16[16,32,512]{2,1,0:T(8,128)(2,1)}, u32[]{:S(2)}, u32[]{:S(2)}) async-start(f16[16,32,512]{2,1,0:T(8,128)(2,1)} %bitcast.36), calls=%async_computation.2 | async-start | bytes 1048576 | tf_op jit(solution)/shard_map/all_to_all | solution.py:62
  171.4 35.1 %copy-start.2 = (s32[512]{0:T(512)S(1)}, s32[512]{0:T(512)}, u32[]{:S(2)}) copy-start(s32[512]{0:T(512)} %param.10) | copy-start | bytes 6148
  174.8 55.8 %copy-start.3 = (s32[64]{0:T(128)S(1)}, s32[64]{0:T(128)}, u32[]{:S(2)}) copy-start(s32[64]{0:T(128)} %param.11) | copy-start | bytes 772
  194.0 35.3 %all-to-all-start.6 = ((f16[16,32,512]{2,1,0:T(8,128)(2,1)}), f16[16,32,512]{2,1,0:T(8,128)(2,1)}, u32[]{:S(2)}, u32[]{:S(2)}) async-start(f16[16,32,512]{2,1,0:T(8,128)(2,1)} %bitcast.35), calls=%async_computation.6 | async-start | bytes 1048576 | tf_op jit(solution)/shard_map/all_to_all | solution.py:62
